TPU v7x, 256 devices: a whole 4x4x8 slice. The times are simulated.
256 devices in a mesh: ctx: 32 (over x, y, core), head: 8 (over z).
Axes of the slice: x: 4, y: 4, z: 8, core: 2. Of those that a mesh axis runs over, the one named last changes fastest.
Arguments:
- queries: bfloat16 [24576, 8192], P('ctx', 'head'), may hold values from -80 to 80
- key_states: bfloat16 [24576, 8192], P('ctx', 'head'), may hold values from -4 to 4
- value_states: bfloat16 [24576, 8192], P('ctx', 'head'), may hold values from -4 to 4
- selection: int32 [512, 2], P('ctx'), may hold values from -1 to 30, as said below
Outputs:
- attended: bfloat16 [24576, 8192], P(('ctx', 'head'))
Inputs may be any that keep to these rules, and one draw needn't show every extreme that they name: For query block b, the rows b * 16 to (b + 1) * 16 - 1 of selection, read row by row, list each of the blocks 0 to b - 1 exactly once in their first b entries, in an order drawn from the seed; all other entries are -1. So no two tiles of one query block list the same key block, and each query block from 1 on lists block 0.
All inputs are finite; a program needn't handle non-finite values.
Results may differ from a plain program's by a relative error of at most 0.0051.
Values may be sent and summed in bfloat16 or wider, within the bound.
A program may use at most 128 MiB of HBM per device.

v0:
```python
import math

import jax
import jax.numpy as jnp
from jax import lax
from jax.sharding import PartitionSpec as P

HEAD_DIM = 128


neg_large = -1e30


def attend(query_rows, key_rows, value_rows, causal):
    scores = jnp.einsum("qhd,khd->hqk", query_rows, key_rows, preferred_element_type=jnp.float32)
    scores = scores * (1.0 / math.sqrt(query_rows.shape[2]))
    if causal:
        row_ids = lax.broadcasted_iota(jnp.int32, scores.shape, 1)
        col_ids = lax.broadcasted_iota(jnp.int32, scores.shape, 2)
        scores = jnp.where(col_ids <= row_ids, scores, neg_large)
    maximum = jnp.max(scores, axis=2, keepdims=True)
    weights = jnp.exp(scores - maximum)
    summed = jnp.sum(weights, axis=2, keepdims=True)
    probabilities = (weights / summed).astype(jnp.bfloat16)
    output = jnp.einsum(
        "hqk,khd->qhd", probabilities, value_rows, preferred_element_type=jnp.float32
    )
    log_total = jnp.transpose(maximum[:, :, 0] + jnp.log(summed[:, :, 0]))
    return (output, log_total)


def combine(own_out, own_log, far_out, far_log, far_live):
    live_mask = far_live[:, :, None, None]
    far_masked = jnp.where(live_mask, far_log, neg_large)
    maximum = jnp.maximum(own_log, jnp.max(far_masked, axis=1))
    own_weight = jnp.exp(own_log - maximum)
    far_weight = jnp.where(live_mask, jnp.exp(far_masked - maximum[:, None]), 0.0)
    numerator = own_weight[..., None] * own_out + jnp.sum(far_weight[..., None] * far_out, axis=1)
    denominator = own_weight + jnp.sum(far_weight, axis=1)
    return numerator / denominator[..., None]


def remote_attend(arrived, key_rows, value_rows):
    senders = arrived.shape[0]
    item_count = arrived.shape[1]
    head_count = arrived.shape[2]
    flat_rows = arrived.reshape(2, senders // 2 * item_count, head_count, arrived.shape[3])

    def one_group(group_rows):
        return attend(group_rows, key_rows, value_rows, False)

    outputs, log_rows = lax.map(one_group, flat_rows)
    far_out = outputs.reshape(arrived.shape).astype(jnp.bfloat16)
    return (far_out, log_rows.reshape(senders, item_count, head_count))


def body(queries, key_states, value_states, selection):
    row_count, row_width = queries.shape
    head_dim = HEAD_DIM
    head_count = row_width // head_dim
    tile_count, pick_count = selection.shape
    tile_len = row_count // tile_count
    senders = lax.axis_size("ctx")
    query_rows = queries.reshape(row_count, head_count, head_dim)
    key_rows = key_states.reshape(row_count, head_count, head_dim)
    value_rows = value_states.reshape(row_count, head_count, head_dim)
    own_out, own_log = attend(query_rows, key_rows, value_rows, True)
    flat_picks = selection.reshape(tile_count * pick_count)
    match_table = (flat_picks[:, None] == jnp.arange(senders, dtype=jnp.int32)[None, :]).astype(
        jnp.bfloat16
    )
    slot_rows = jnp.repeat(queries.reshape(tile_count, tile_len * row_width), pick_count, axis=0)
    outgoing = jnp.einsum("sp,sx->px", match_table, slot_rows, preferred_element_type=jnp.float32)
    outgoing = outgoing.astype(jnp.bfloat16).reshape(senders, tile_len, head_count, head_dim)
    arrived = lax.all_to_all(outgoing, "ctx", split_axis=0, concat_axis=0, tiled=True)
    far_out, far_log = remote_attend(arrived, key_rows, value_rows)
    back_out = lax.all_to_all(far_out, "ctx", split_axis=0, concat_axis=0, tiled=True)
    back_log = lax.all_to_all(far_log, "ctx", split_axis=0, concat_axis=0, tiled=True)
    safe_index = jnp.clip(flat_picks, 0, senders - 1)
    mine_out = (
        jnp.take(back_out, safe_index, axis=0)
        .astype(jnp.float32)
        .reshape(tile_count, pick_count, tile_len, head_count, head_dim)
    )
    mine_log = jnp.take(back_log, safe_index, axis=0).reshape(
        tile_count, pick_count, tile_len, head_count
    )
    combined = combine(
        own_out.reshape(tile_count, tile_len, head_count, head_dim),
        own_log.reshape(tile_count, tile_len, head_count),
        mine_out,
        mine_log,
        selection >= 0,
    )
    attended = combined.astype(jnp.bfloat16).reshape(row_count, row_width)
    return lax.all_to_all(attended, "head", split_axis=0, concat_axis=1, tiled=True)


def solution(mesh):
    placed = (P("ctx", "head"), P("ctx", "head"), P("ctx", "head"), P("ctx", None))
    return jax.shard_map(
        body, mesh=mesh, in_specs=placed, out_specs=P(("ctx", "head"), None), check_vma=False
    )
```

profile of v0, /device:TPU:2, one launch (start us, length us, event | category | flops | bytes accessed | tf_op | source)
XLA Modules:
  0.0 248.6 jit_solution(17589617309919166353)
XLA Ops:
  0.0 1.9 reshape.129
  1.9 4.3 %broadcast_in_dim.74 = bf16[16,2,49152]{2,1,0:T(2,128)(2,1)} broadcast(bf16[16,49152]{1,0:T(8,128)(2,1)S(1)} %reshape.129), dimensions={0,2} | broadcast | bytes 4718592 | tf_op jit(solution)/shard_map/broadcast_in_dim | solution.py:72
  6.2 3.3 %reshape.130 = bf16[32,49152]{1,0:T(8,128)(2,1)S(1)} reshape(bf16[16,2,49152]{2,1,0:T(2,128)(2,1)} %broadcast_in_dim.74) | data formatting | bytes 6291456 | tf_op jit(solution)/shard_map/reshape | solution.py:72
  10.7 2.4 copy.124
  13.1 7.8 %all-to-all-start = ((bf16[32,48,8,128]{3,2,1,0:T(8,128)(2,1)}), bf16[32,48,8,128]{3,2,1,0:T(8,128)(2,1)}, u32[]{:S(2)}, u32[]{:S(2)}) async-start(bf16[32,48,8,128]{3,2,1,0:T(8,128)(2,1)} %bitcast.24), calls=%async_computation | async-start | bytes 6291456 | tf_op jit(solution)/shard_map/all_to_all | solution.py:75
  23.8 1.7 copy.92
  27.7 11.0 %fusion.6 = (f32[8,768]{1,0:T(8,128)S(1)}, f32[8,768,768]{1,2,0:T(8,128)}) fusion(bf16[768,8,128]{0,2,1:T(8,128)(2,1)} %bitcast.78, bf16[768,1024]{1,0:T(8,128)(2,1)} %param.6), kind=kOutput, calls=%fused_computation.20 | convolution fusion | flops 1226827776 | bytes 22044672 | tf_op jit(solution)/shard_map/qhd,khd->hqk/dot_general | solution.py:15
  38.8 8.7 %fusion.5 = f32[8,768]{1,0:T(8,128)S(1)} fusion(f32[8,768,768]{1,2,0:T(8,128)} %get-tuple-element.85, f32[8,768]{1,0:T(8,128)S(1)} %get-tuple-element.84), kind=kLoop, calls=%fused_computation.19 | loop fusion | flops 23586816 | bytes 18923520 | tf_op jit(solution)/shard_map/reduce_sum | solution.py:23
  48.1 10.2 %all-to-all-done = bf16[32,48,8,128]{3,2,1,0:T(8,128)(2,1)} async-done(((bf16[32,48,8,128]{3,2,1,0:T(8,128)(2,1)}), bf16[32,48,8,128]{3,2,1,0:T(8,128)(2,1)}, u32[]{:S(2)}, u32[]{:S(2)}) %all-to-all-start) | async-done | bytes 3145760 | tf_op jit(solution)/shard_map/all_to_all | solution.py:75
  58.3 62.0 %while.12 = (s32[]{:T(128)}, bf16[2,768,8,128]{3,2,1,0:T(8,128)(2,1)}, f32[2,768,8]{1,0,2:T(2,128)S(1)}, bf16[2,768,8,128]{3,2,1,0:T(8,128)(2,1)}, bf16[768,8,12...) while((s32[]{:T(128)}, bf16[2,768,8,128]{3,2,1,0:T(8,128)(2,1)}, ...), condition=%wide.region_5.6_spmd, body=%wide.region_2.5_spmd.sunk | while | flops 2458380288 | bytes 94666904 | solution.py:52
  60.0 7.9 %multiply_reduce_fusion.3 = (f32[8,768]{1,0:T(8,128)S(1)}, f32[8,768,768]{1,2,0:T(8,128)}) fusion(bf16[768,8,128]{2,0,1:T(8,128)(2,1)S(1)} %get-tuple-element.147, bf16[1,768,8,128]{3,2,1,0:T(8,128)(2,1)S(1)} %constant_dynamic-slice_fusion.2), kind=kOutput, calls=%fused_computation.4.clone.1 | convolution fusion | flops 1217390592 | bytes 22044672 | tf_op jit(solution)/shard_map/while/body/eval_jaxpr/qhd,khd->hqk/dot_general | solution.py:15
  67.9 9.4 %fusion.32 = f32[8,768]{1,0:T(8,128)S(1)} fusion(f32[8,768,768]{1,2,0:T(8,128)} %get-tuple-element.125, f32[8,768]{1,0:T(8,128)S(1)} %get-tuple-element.126), kind=kLoop, calls=%fused_computation.5.clone.1 | loop fusion | flops 14149632 | bytes 18923520 | tf_op jit(solution)/shard_map/while/body/eval_jaxpr/reduce_sum | solution.py:23
  77.4 9.1 %fusion.33 = bf16[1,768,8,128]{3,1,2,0:T(8,128)(2,1)S(1)} fusion(bf16[768,8,128]{2,0,1:T(8,128)(2,1)S(1)} %get-tuple-element.148, f32[8,768,768]{1,2,0:T(8,128)} %get-tuple-element.125, f32[8,768]{1,0:T(8,128)S(1)} %fusion.32, f32[8,768]{1,0:T(8,128)S(1)} %get-tuple-element.126), kind=kOutput, calls=%fused_computation.8.clone.1 | convolution fusion | flops 1226833920 | bytes 22069248 | tf_op jit(solution)/shard_map/while/body/eval_jaxpr/hqk,khd->qhd/dot_general | solution.py:25
  90.9 7.9 %multiply_reduce_fusion.3 = (f32[8,768]{1,0:T(8,128)S(1)}, f32[8,768,768]{1,2,0:T(8,128)}) fusion(bf16[768,8,128]{2,0,1:T(8,128)(2,1)S(1)} %get-tuple-element.147, bf16[1,768,8,128]{3,2,1,0:T(8,128)(2,1)S(1)} %constant_dynamic-slice_fusion.2), kind=kOutput, calls=%fused_computation.4.clone.1 | convolution fusion | flops 1217390592 | bytes 22044672 | tf_op jit(solution)/shard_map/while/body/eval_jaxpr/qhd,khd->hqk/dot_general | solution.py:15
  98.8 9.4 %fusion.32 = f32[8,768]{1,0:T(8,128)S(1)} fusion(f32[8,768,768]{1,2,0:T(8,128)} %get-tuple-element.125, f32[8,768]{1,0:T(8,128)S(1)} %get-tuple-element.126), kind=kLoop, calls=%fused_computation.5.clone.1 | loop fusion | flops 14149632 | bytes 18923520 | tf_op jit(solution)/shard_map/while/body/eval_jaxpr/reduce_sum | solution.py:23
  108.3 9.1 %fusion.33 = bf16[1,768,8,128]{3,1,2,0:T(8,128)(2,1)S(1)} fusion(bf16[768,8,128]{2,0,1:T(8,128)(2,1)S(1)} %get-tuple-element.148, f32[8,768,768]{1,2,0:T(8,128)} %get-tuple-element.125, f32[8,768]{1,0:T(8,128)S(1)} %fusion.32, f32[8,768]{1,0:T(8,128)S(1)} %get-tuple-element.126), kind=kOutput, calls=%fused_computation.8.clone.1 | convolution fusion | flops 1226833920 | bytes 22069248 | tf_op jit(solution)/shard_map/while/body/eval_jaxpr/hqk,khd->qhd/dot_general | solution.py:25
  121.3 7.4 %all-to-all-start.1 = ((f32[32,1,384]{2,1,0:T(1,128)}), f32[32,1,384]{2,1,0:T(1,128)S(1)}, u32[]{:S(2)}, u32[]{:S(2)}) async-start(f32[32,1,384]{2,1,0:T(1,128)} %reshape.152), calls=%async_computation.1 | async-start | bytes 98304 | tf_op jit(solution)/shard_map/all_to_all | solution.py:78
  129.3 5.8 %all-to-all-done.1 = f32[32,1,384]{2,1,0:T(1,128)S(1)} async-done(((f32[32,1,384]{2,1,0:T(1,128)}), f32[32,1,384]{2,1,0:T(1,128)S(1)}, u32[]{:S(2)}, u32[]{:S(2)}) %all-to-all-start.1) | async-done | bytes 49184 | tf_op jit(solution)/shard_map/all_to_all | solution.py:78
  135.1 6.0 %all-to-all-start.2 = ((bf16[32,48,8,128]{3,2,1,0:T(8,128)(2,1)}), bf16[32,48,8,128]{3,2,1,0:T(8,128)(2,1)}, u32[]{:S(2)}, u32[]{:S(2)}) async-start(bf16[32,48,8,128]{3,2,1,0:T(8,128)(2,1)} %bitcast.80), calls=%async_computation.2 | async-start | bytes 6291456 | tf_op jit(solution)/shard_map/all_to_all | solution.py:77
  141.1 8.5 %fusion.9 = f32[768,8,128]{2,0,1:T(8,128)S(1)} fusion(bf16[768,8,128]{0,2,1:T(8,128)(2,1)S(1)} %bitcast.76, f32[8,768,768]{1,2,0:T(8,128)} %get-tuple-element.85, f32[8,768]{1,0:T(8,128)S(1)} %copy-done.12, f32[8,768]{1,0:T(8,128)S(1)} %copy-done.10), kind=kOutput, calls=%fused_computation.25 | convolution fusion | flops 1236271104 | bytes 23642112 | tf_op jit(solution)/shard_map/hqk,khd->qhd/dot_general | solution.py:25
  149.7 3.5 %copy.104 = f32[768,8,128]{2,1,0:T(8,128)} copy(f32[768,8,128]{2,0,1:T(8,128)S(1)} %fusion.9) | data formatting | bytes 6291456 | tf_op jit(solution)/shard_map/hqk,khd->qhd/transpose | solution.py:25
  153.1 2.8 %reshape.135 = f32[8,96,1024]{2,1,0:T(8,128)S(1)} reshape(f32[768,8,128]{2,1,0:T(8,128)} %copy.104) | data formatting | bytes 6291456 | tf_op jit(solution)/shard_map/reshape | solution.py:89
  160.6 2.2 div.30
  162.8 4.6 %div.31 = f32[8,96,1024]{2,1,0:T(8,128)} reshape(f32[16,48,8,128]{3,2,1,0:T(8,128)} %div.30) | data formatting | bytes 6291456 | tf_op jit(solution)/shard_map/div | solution.py:40
  169.6 2.2 mul.27
  171.8 4.6 %mul.28 = f32[8,96,1024]{2,1,0:T(8,128)} reshape(f32[16,48,8,128]{3,2,1,0:T(8,128)} %mul.27) | data formatting | bytes 6291456 | tf_op jit(solution)/shard_map/mul | solution.py:38
  176.4 2.3 all-to-all-done.2
  178.7 4.5 %gather_fusion.1 = bf16[32,48,8,128]{3,2,1,0:T(8,128)(2,1)} fusion(bf16[32,48,8,128]{3,2,1,0:T(8,128)(2,1)} %all-to-all-done.2, s32[1024]{0:T(1024)S(1)} %pad_clamp_fusion), kind=kCustom, calls=%fused_computation.1 | custom fusion | bytes 6291584 | tf_op jit(solution)/shard_map/jit(_take)/gather | solution.py:81
  183.2 5.8 %multiply_reduce_fusion.1 = f32[16,48,8,128]{3,2,1,0:T(8,128)} fusion(f32[16,2,48,8]{3,2,1,0:T(8,128)} %copy.105, pred[16,2]{1,0:T(8,128)(4,1)S(1)} %copy.90, bf16[32,48,8,128]{3,2,1,0:T(8,128)(2,1)} %gather_fusion.1), kind=kLoop, calls=%fused_computation.22 | loop fusion | flops 5505024 | bytes 6340640 | tf_op jit(solution)/shard_map/reduce_sum | solution.py:38
  189.1 4.6 %reduce_sum.40 = f32[8,96,1024]{2,1,0:T(8,128)} reshape(f32[16,48,8,128]{3,2,1,0:T(8,128)} %multiply_reduce_fusion.1) | data formatting | bytes 6291456 | tf_op jit(solution)/shard_map/reduce_sum | solution.py:38
  193.7 5.2 %divide_convert_fusion.6 = bf16[8,96,1024]{2,1,0:T(8,128)(2,1)S(1)} fusion(f32[8,96,1024]{2,1,0:T(8,128)} %div.31, f32[8,96,1024]{2,1,0:T(8,128)} %reduce_sum.40, f32[8,96,1024]{2,1,0:T(8,128)} %mul.28, f32[8,96,1024]{2,1,0:T(8,128)S(1)} %reshape.135), kind=kLoop, calls=%fused_computation.23 | loop fusion | flops 3145728 | bytes 14155776 | tf_op jit(solution)/shard_map/convert_element_type | solution.py:95
  198.9 48.4 %all_to_all.31 = bf16[8,96,1024]{2,1,0:T(8,128)(2,1)S(1)} all-to-all(bf16[8,96,1024]{2,1,0:T(8,128)(2,1)S(1)} %divide_convert_fusion.6), channel_id=1, replica_groups=mesh['ctx'=32,'head'=8] {'head'}, dimensions={0} | all-to-all | bytes 3145728 | tf_op jit(solution)/shard_map/all_to_all | solution.py:96
  (79 shorter events, 25.4 us)
Async XLA Ops:
  6.2 3.3 %copy-start.13 = (s32[16,2]{0,1:T(2,128)S(1)}, s32[16,2]{0,1:T(2,128)}, u32[]{:S(2)}) copy-start(s32[16,2]{0,1:T(2,128)} %param.9) | copy-start | bytes 388
  13.1 7.8 %copy-start.5 = (bf16[768,1024]{1,0:T(8,128)(2,1)S(1)}, bf16[768,1024]{1,0:T(8,128)(2,1)}, u32[]{:S(2)}) copy-start(bf16[768,1024]{1,0:T(8,128)(2,1)} %param.7) | copy-start | bytes 4718596
  13.1 45.2 %all-to-all-start = ((bf16[32,48,8,128]{3,2,1,0:T(8,128)(2,1)}), bf16[32,48,8,128]{3,2,1,0:T(8,128)(2,1)}, u32[]{:S(2)}, u32[]{:S(2)}) async-start(bf16[32,48,8,128]{3,2,1,0:T(8,128)(2,1)} %bitcast.24), calls=%async_computation | async-start | bytes 6291456 | tf_op jit(solution)/shard_map/all_to_all | solution.py:75
  21.6 1.2 copy-start.2
  25.5 13.3 %copy-start = (bf16[768,1024]{0,1:T(8,128)(2,1)}, bf16[768,1024]{0,1:T(8,128)(2,1)S(1)}, u32[]{:S(2)}) copy-start(bf16[768,1024]{0,1:T(8,128)(2,1)S(1)} %copy.92) | copy-start | bytes 4718596
  38.8 8.7 %copy-start.9 = (f32[8,768]{1,0:T(8,128)}, f32[8,768]{1,0:T(8,128)S(1)}, u32[]{:S(2)}) copy-start(f32[8,768]{1,0:T(8,128)S(1)} %get-tuple-element.84) | copy-start | bytes 73732
  38.8 19.5 %copy-start.6 = (bf16[768,8,128]{2,0,1:T(8,128)(2,1)S(1)}, bf16[768,8,128]{2,0,1:T(8,128)(2,1)}, u32[]{:S(2)}) copy-start(bf16[768,8,128]{2,0,1:T(8,128)(2,1)} %copy.95) | copy-start | bytes 4718596
  47.5 10.8 %copy-start.11 = (f32[8,768]{1,0:T(8,128)}, f32[8,768]{1,0:T(8,128)S(1)}, u32[]{:S(2)}) copy-start(f32[8,768]{1,0:T(8,128)S(1)} %fusion.5) | copy-start | bytes 73732
  58.3 70.5 %copy-start.14 = (s32[16,2]{0,1:T(2,128)S(1)}, s32[16,2]{0,1:T(2,128)}, u32[]{:S(2)}) copy-start(s32[16,2]{0,1:T(2,128)} %param.9) | copy-start | bytes 388
  58.3 70.5 %copy-start.15 = (s32[16,2]{0,1:T(2,128)S(1)}, s32[16,2]{0,1:T(2,128)}, u32[]{:S(2)}) copy-start(s32[16,2]{0,1:T(2,128)} %broadcast_clamp_fusion) | copy-start | bytes 388
  58.3 70.9 %copy-start.8 = (f32[768,8]{0,1:T(8,128)S(1)}, f32[768,8]{0,1:T(8,128)}, u32[]{:S(2)}) copy-start(f32[768,8]{0,1:T(8,128)} %add_bitcast_fusion.1) | copy-start | bytes 73732
  77.4 9.1 %copy-start.3 = (bf16[2,768,8,128]{3,2,1,0:T(8,128)(2,1)S(1)}, bf16[2,768,8,128]{3,2,1,0:T(8,128)(2,1)}, u32[]{:S(2)}) copy-start(bf16[2,768,8,128]{3,2,1,0:T(8,128)(2,1)} %get-tuple-element.136) | copy-start | bytes 9437188 | tf_op jit(solution)/shard_map/while
  87.6 1.7 copy-start.4
  108.3 9.1 %copy-start.3 = (bf16[2,768,8,128]{3,2,1,0:T(8,128)(2,1)S(1)}, bf16[2,768,8,128]{3,2,1,0:T(8,128)(2,1)}, u32[]{:S(2)}) copy-start(bf16[2,768,8,128]{3,2,1,0:T(8,128)(2,1)} %get-tuple-element.136) | copy-start | bytes 9437188 | tf_op jit(solution)/shard_map/while
  118.5 1.7 copy-start.4
  121.3 13.7 %all-to-all-start.1 = ((f32[32,1,384]{2,1,0:T(1,128)}), f32[32,1,384]{2,1,0:T(1,128)S(1)}, u32[]{:S(2)}, u32[]{:S(2)}) async-start(f32[32,1,384]{2,1,0:T(1,128)} %reshape.152), calls=%async_computation.1 | async-start | bytes 98304 | tf_op jit(solution)/shard_map/all_to_all | solution.py:78
  135.1 6.0 %copy-start.1 = (bf16[768,1024]{0,1:T(8,128)(2,1)S(1)}, bf16[768,1024]{0,1:T(8,128)(2,1)}, u32[]{:S(2)}) copy-start(bf16[768,1024]{0,1:T(8,128)(2,1)} %copy-done) | copy-start | bytes 4718596
  135.1 6.0 %copy-start.10 = (f32[8,768]{1,0:T(8,128)S(1)}, f32[8,768]{1,0:T(8,128)}, u32[]{:S(2)}) copy-start(f32[8,768]{1,0:T(8,128)} %copy-done.9) | copy-start | bytes 73732
  135.1 6.0 %copy-start.12 = (f32[8,768]{1,0:T(8,128)S(1)}, f32[8,768]{1,0:T(8,128)}, u32[]{:S(2)}) copy-start(f32[8,768]{1,0:T(8,128)} %copy-done.11) | copy-start | bytes 73732
  135.1 43.6 %all-to-all-start.2 = ((bf16[32,48,8,128]{3,2,1,0:T(8,128)(2,1)}), bf16[32,48,8,128]{3,2,1,0:T(8,128)(2,1)}, u32[]{:S(2)}, u32[]{:S(2)}) async-start(bf16[32,48,8,128]{3,2,1,0:T(8,128)(2,1)} %bitcast.80), calls=%async_computation.2 | async-start | bytes 6291456 | tf_op jit(solution)/shard_map/all_to_all | solution.py:77
  162.8 4.6 %copy-start.7 = (f32[16,2,48,8]{2,3,1,0:T(8,128)S(1)}, f32[16,2,48,8]{2,3,1,0:T(8,128)}, u32[]{:S(2)}) copy-start(f32[16,2,48,8]{2,3,1,0:T(8,128)} %get-tuple-element.79) | copy-start | bytes 147460
where the time goes:
time: 251 us; the launch traced here: 249 us
  local copies, waits for them, and re-layouts  63.1 us (25%)
  matrix products  54.6 us (22%)
  blocking collectives  48.4 us (19%)
  other arithmetic  42.4 us (17%)
  starting transfers between devices  21.2 us (8%)
  waiting for transfers between devices  18.3 us (7%)
    all_to_all x1, blocking collectives, body(): lax.all_to_all(attended, 'head', split_axis=0, concat_axis=1, tiled=True)  48.4 us
    reduce_sum x3, other arithmetic, attend(): summed = jnp.sum(weights, axis=2, keepdims=True)  27.6 us
    dot_general x3, matrix products, attend(): jnp.einsum('qhd,khd->hqk', query_rows, key_rows, preferred_element_type=j...  26.8 us
    dot_general x3, matrix products, attend(): jnp.einsum('hqk,khd->qhd', probabilities, value_rows, preferred_element_t...  26.6 us
    all_to_all x1, waiting for transfers between devices, body(): lax.all_to_all(outgoing, 'ctx', split_axis=0, concat_axis=0, tiled=True)  10.2 us
    all_to_all x1, starting transfers between devices, body(): lax.all_to_all(outgoing, 'ctx', split_axis=0, concat_axis=0, tiled=True)  7.8 us
    all_to_all x1, starting transfers between devices, body(): lax.all_to_all(far_log, 'ctx', split_axis=0, concat_axis=0, tiled=True)  7.42 us
    unnamed x34, local copies, waits for them, and re-layouts  6.98 us
  transfers between devices with their start and end apart: 3, of which 3 were waited for; matrix products, arithmetic and copies ran while one was open for 25% of the time, Pallas kernels for 0%

commit v1 on v0

v1 whole, which is shorter than its diff:
```python
import functools
import math

import jax
import jax.numpy as jnp
from jax import lax
from jax.experimental import pallas as pl
from jax.experimental.pallas import tpu as pltpu
from jax.sharding import PartitionSpec as P

HEAD_DIM = 128
TILE = 48
GROUP = 4
UNIT = 16
ROWS = 128
LAG = 2
AHEAD = 2
FLIGHT = 1
NEG = -1e30
SCALE2 = math.log2(math.e) / math.sqrt(HEAD_DIM)
MESH = pl.DeviceIdType.MESH


def loop(low, high, step):
    def once(i, carry):
        step(i)
        return carry

    lax.fori_loop(low, high, once, 0)


def softmax_parts(scores, values):
    top = jnp.max(scores, axis=1, keepdims=True)
    weights = jnp.exp2((scores - top) * SCALE2).astype(jnp.bfloat16)
    summed = jnp.dot(weights, values, preferred_element_type=jnp.float32)
    total = summed[:, HEAD_DIM:]
    return summed[:, :HEAD_DIM] / total, top * SCALE2 + jnp.log2(total)


def kernel(
    blocks, depth, sel, q, k_hbm, v_hbm, out,
    k, outgoing, arrived, parts, part_lse, back, back_lse, own, own_lse, final, vext, going, onehot, pick, dead, picked_lse,
    fwd_send, fwd_recv, out_send, out_recv, lse_send, lse_recv, z_send, z_recv, load_sem,
):
    me, z = lax.axis_index("ctx"), lax.axis_index("head")
    rows, width = q.shape
    heads = width // HEAD_DIM
    tiles = rows // TILE
    share = rows // depth

    barrier = pltpu.get_barrier_semaphore()
    loop(1, blocks, lambda i: pl.semaphore_signal(
        barrier, inc=1, device_id=(lax.rem(me + i, blocks), z), device_id_type=MESH))
    loop(1, depth, lambda i: pl.semaphore_signal(
        barrier, inc=1, device_id=(me, lax.rem(z + i, depth)), device_id_type=MESH))

    def columns(h):
        return pl.ds(pl.multiple_of(h * HEAD_DIM, HEAD_DIM), HEAD_DIM)

    load_k = pltpu.make_async_copy(k_hbm, k, load_sem.at[heads])
    load_v = [
        pltpu.make_async_copy(
            v_hbm.at[:, h * HEAD_DIM:(h + 1) * HEAD_DIM], vext.at[h, :, :HEAD_DIM], load_sem.at[h])
        for h in range(heads)
    ]
    for copy in [load_k] + load_v:
        copy.start()

    def shifted(size):
        return (lax.broadcasted_iota(jnp.int32, (TILE, size), 1)
                - lax.broadcasted_iota(jnp.int32, (TILE, size), 0))

    lanes = lax.broadcasted_iota(jnp.int32, (1, HEAD_DIM), 1)

    def choose(c):
        tile = jnp.int32(0)
        for t in range(tiles):
            tile += jnp.where((sel[t, 0] == c) | (sel[t, 1] == c), t, 0)
        here = pl.ds(pl.multiple_of(c * TILE, 16), TILE)
        going[here] = jnp.where(shifted(rows) == tile * TILE, 1.0, 0.0).astype(jnp.bfloat16)

    def select(t):
        for r in range(2):
            i, c = 2 * t + r, sel[t, r]
            here = pl.ds(pl.multiple_of(i * TILE, 16), TILE)
            onehot[here] = jnp.where(shifted(blocks * TILE) == c * TILE, 1.0, 0.0).astype(jnp.bfloat16)
            pick[pl.ds(i, 1)] = jnp.where(lanes == c, 1.0, 0.0)
            dead[pl.ds(i, 1)] = jnp.where(lanes * 0 + c < 0, NEG, 0.0)

    slots = 2 * GROUP
    quads = (me + slots - 1) // slots

    def gather(h):
        def one_quad(j):
            here = pl.ds(pl.multiple_of(j * slots * TILE, 16), slots * TILE)
            tiles_out = jnp.dot(going[here], q[:, columns(h)], preferred_element_type=jnp.float32)
            outgoing[h, pl.ds(j * slots, slots)] = tiles_out.astype(jnp.bfloat16).reshape(slots, TILE, HEAD_DIM)

        loop(0, quads, one_quad)

    loop(0, quads * slots, choose)
    loop(0, FLIGHT, gather)
    loop(0, quads * GROUP, select)

    def clear(c):
        for h in range(heads):
            back[h, c] = jnp.zeros((TILE, HEAD_DIM), jnp.bfloat16)
            back_lse[h, c] = jnp.zeros((1, HEAD_DIM), jnp.float32)

    loop(me, blocks, clear)

    for h in range(heads):
        vext[h, :, HEAD_DIM:] = jnp.ones((rows, HEAD_DIM), jnp.bfloat16)
    for copy in [load_k] + load_v:
        copy.wait()

    pl.semaphore_wait(barrier, blocks - 1 + depth - 1)

    def forward(h, c, slot):
        return pltpu.make_async_remote_copy(
            src_ref=outgoing.at[h, c], dst_ref=arrived.at[h, slot],
            send_sem=fwd_send.at[c], recv_sem=fwd_recv.at[h, slot],
            device_id=(c, z), device_id_type=MESH)

    def backward(h, b, slot):
        return pltpu.make_async_remote_copy(
            src_ref=parts.at[h, b], dst_ref=back.at[h, slot],
            send_sem=out_send.at[b], recv_sem=out_recv.at[h, slot],
            device_id=(b, z), device_id_type=MESH)

    def backward_lse(h, b, slot):
        return pltpu.make_async_remote_copy(
            src_ref=part_lse.at[h, b], dst_ref=back_lse.at[h, slot],
            send_sem=lse_send.at[b], recv_sem=lse_recv.at[h, slot],
            device_id=(b, z), device_id_type=MESH)

    def across(h, d):
        other = lax.rem(z + d, depth)
        return pltpu.make_async_remote_copy(
            src_ref=final.at[h, pl.ds(pl.multiple_of(other * share, 16), share)],
            dst_ref=out.at[:, columns(z * heads + h)],
            send_sem=z_send.at[h], recv_sem=z_recv.at[h],
            device_id=(me, other), device_id_type=MESH)

    def send_tiles(h):
        @pl.when(h > 0)
        def _():
            loop(0, me, lambda c: forward(h - 1, c, me).wait_send())

        loop(0, me, lambda i: forward(h, me - 1 - i, me).start())

    def parts_sent(h, low, high):
        def sent(b):
            backward(h, b, me).wait_send()
            backward_lse(h, b, me).wait_send()

        loop(low, high, sent)

    loop(0, FLIGHT, send_tiles)

    def attend_own(h):
        for r in range(rows // ROWS):
            low, high = r * ROWS, (r + 1) * ROWS
            scores = lax.dot_general(
                q[low:high, columns(h)], k[:high, columns(h)], (((1,), (1,)), ((), ())),
                preferred_element_type=jnp.float32)
            row_ids = low + lax.broadcasted_iota(jnp.int32, scores.shape, 0)
            col_ids = lax.broadcasted_iota(jnp.int32, scores.shape, 1)
            scores = jnp.where(col_ids <= row_ids, scores, NEG)
            own[h, low:high], own_lse[h, low:high] = softmax_parts(scores, vext[h, :high])

    lane = lax.broadcasted_iota(jnp.int32, (TILE, HEAD_DIM), 1)
    row = lax.broadcasted_iota(jnp.int32, (TILE, HEAD_DIM), 0)
    diagonal = lane == row

    def attend_far(h):
        loop(me + 1, blocks, lambda b: forward(h, b, b).wait_recv())

        @pl.when(h > 0)
        def _():
            parts_sent(h - 1, me + 1, blocks)

        def one_group(first):
            queries = arrived[h, pl.ds(first, GROUP)].reshape(GROUP * TILE, HEAD_DIM)
            scores = lax.dot_general(
                queries, k[:, columns(h)], (((1,), (1,)), ((), ())),
                preferred_element_type=jnp.float32)
            output, lse = softmax_parts(scores, vext[h])
            parts[h, pl.ds(first, GROUP)] = output.astype(jnp.bfloat16).reshape(GROUP, TILE, HEAD_DIM)
            for j in range(GROUP):
                part_lse[h, first + j] = jnp.sum(
                    jnp.where(diagonal, lse[j * TILE:(j + 1) * TILE], 0.0), axis=0, keepdims=True)

        def one_unit(i):
            first = blocks - UNIT * (i + 1)
            for g in range(UNIT // GROUP):
                one_group(first + g * GROUP)

            def send(b):
                backward(h, b, me).start()
                backward_lse(h, b, me).start()

            loop(jnp.maximum(first, me + 1), first + UNIT, send)

        loop(0, (blocks - 1 - me + UNIT - 1) // UNIT, one_unit)

    def combine(h):
        def arrive(c):
            backward(h, c, c).wait_recv()
            backward_lse(h, c, c).wait_recv()

        loop(0, me, arrive)
        picked_lse[...] = dead[...] + jnp.dot(
            pick[:, :blocks], back_lse[h].reshape(blocks, HEAD_DIM),
            precision=lax.Precision.HIGHEST, preferred_element_type=jnp.float32)

        def with_far(j):
            got = jnp.dot(
                onehot[pl.ds(pl.multiple_of(j * slots * TILE, 16), slots * TILE)],
                back[h].reshape(blocks * TILE, HEAD_DIM), preferred_element_type=jnp.float32)
            for t in range(GROUP):
                here = pl.ds(pl.multiple_of((GROUP * j + t) * TILE, 16), TILE)
                outputs, lses = [own[h, here]], [own_lse[h, here]]
                for r in range(2):
                    i = 2 * t + r
                    outputs.append(got[i * TILE:(i + 1) * TILE])
                    spread = jnp.where(diagonal, picked_lse[pl.ds(slots * j + i, 1)], 0.0)
                    lses.append(jnp.sum(spread, axis=1, keepdims=True))
                top = jnp.maximum(jnp.maximum(lses[0], lses[1]), lses[2])
                weights = [jnp.exp2(lse - top) for lse in lses]
                numerator = weights[0] * outputs[0] + weights[1] * outputs[1] + weights[2] * outputs[2]
                final[h, here] = (numerator / (weights[0] + weights[1] + weights[2])).astype(jnp.bfloat16)

        def alone(j):
            here = pl.ds(pl.multiple_of(j * GROUP * TILE, 16), GROUP * TILE)
            final[h, here] = own[h, here].astype(jnp.bfloat16)

        loop(0, quads, with_far)
        loop(quads, tiles // GROUP, alone)
        for d in range(1, depth):
            across(h, d).start()
        out[:, columns(z * heads + h)] = final[h, pl.ds(pl.multiple_of(z * share, 16), share)]

    loop(0, AHEAD, attend_own)

    def one_step(h):
        @pl.when(h + FLIGHT < heads)
        def _():
            gather(h + FLIGHT)
            send_tiles(h + FLIGHT)

        @pl.when(h < heads)
        def _():
            attend_far(h)

        @pl.when(h + AHEAD < heads)
        def _():
            attend_own(h + AHEAD)

        @pl.when(h >= LAG)
        def _():
            combine(h - LAG)

    loop(0, heads + LAG, one_step)

    loop(0, me, lambda c: forward(heads - 1, c, me).wait_send())
    parts_sent(heads - 1, me + 1, blocks)

    def drain(h):
        shares = final.at[h, :(depth - 1) * share]
        pltpu.make_async_copy(shares, shares, z_send.at[h]).wait()
        pltpu.make_async_copy(shares, shares, z_recv.at[h]).wait()

    loop(0, heads, drain)


def body(blocks, depth, queries, key_states, value_states, selection):
    rows, width = queries.shape
    heads = width // HEAD_DIM
    bf16, f32 = jnp.bfloat16, jnp.float32
    tile_set = pltpu.VMEM((heads, blocks, TILE, HEAD_DIM), bf16)
    lse_set = pltpu.VMEM((heads, blocks, 1, HEAD_DIM), f32)
    dma = pltpu.SemaphoreType.DMA
    vmem, anywhere = pl.BlockSpec(memory_space=pltpu.VMEM), pl.BlockSpec(memory_space=pl.ANY)
    return pl.pallas_call(
        functools.partial(kernel, blocks, depth),
        out_shape=jax.ShapeDtypeStruct((rows // depth, width * depth), bf16),
        in_specs=[pl.BlockSpec(memory_space=pltpu.SMEM), vmem, anywhere, anywhere],
        out_specs=vmem,
        scratch_shapes=[
            pltpu.VMEM((rows, width), bf16),
            tile_set, tile_set, tile_set, lse_set, tile_set, lse_set,
            pltpu.VMEM((heads, rows, HEAD_DIM), f32),
            pltpu.VMEM((heads, rows, HEAD_DIM), f32),
            pltpu.VMEM((heads, rows, HEAD_DIM), bf16),
            pltpu.VMEM((heads, rows, 2 * HEAD_DIM), bf16),
            pltpu.VMEM((blocks * TILE, rows), bf16),
            pltpu.VMEM((blocks * TILE, blocks * TILE), bf16),
            pltpu.VMEM((blocks, HEAD_DIM), f32),
            pltpu.VMEM((blocks, HEAD_DIM), f32),
            pltpu.VMEM((blocks, HEAD_DIM), f32),
            dma((blocks,)), dma((heads, blocks)), dma((blocks,)), dma((heads, blocks)),
            dma((blocks,)), dma((heads, blocks)), dma((heads,)), dma((heads,)),
            dma((heads + 1,)),
        ],
        compiler_params=pltpu.CompilerParams(
            collective_id=0, has_side_effects=True, vmem_limit_bytes=56 * 2**20),
    )(selection, queries, key_states, value_states)


def solution(mesh):
    placed = (P("ctx", "head"), P("ctx", "head"), P("ctx", "head"), P("ctx", None))
    return jax.shard_map(
        functools.partial(body, mesh.shape["ctx"], mesh.shape["head"]),
        mesh=mesh, in_specs=placed, out_specs=P(("ctx", "head"), None), check_vma=False)
```

time: 251 us -> 96.2 us (0.38)
  Pallas kernels: 0 us -> 92 us
  local copies, waits for them, and re-layouts: 63.1 us -> 4 us
  matrix products: 54.6 us -> 0 us
  blocking collectives: 48.4 us -> 0 us
  other arithmetic: 42.4 us -> 0 us
  starting transfers between devices: 21.2 us -> 0 us
  waiting for transfers between devices: 18.3 us -> 0 us
    pallas_call x0 -> x1, Pallas kernels: none -> 92 us  [body(): pl.pallas_call(functools.partial(kernel, blocks, depth), out_shape=jax.Sh...]
    dot_general x7 -> x0, matrix products: 54.6 us -> none  [the longest x3 26.8 us: attend(): jnp.einsum('qhd,khd->hqk', query_rows, key_rows, preferred_element_type=j...]
    all_to_all x1 -> x0, blocking collectives: 48.4 us -> none  [body(): lax.all_to_all(attended, 'head', split_axis=0, concat_axis=1, tiled=True)]
    reduce_sum x5 -> x0, other arithmetic: 34.2 us -> none  [the longest x3 27.6 us: attend(): summed = jnp.sum(weights, axis=2, keepdims=True)]
    all_to_all x3 -> x0, starting transfers between devices: 21.2 us -> none  [the longest x1 7.8 us: body(): lax.all_to_all(outgoing, 'ctx', split_axis=0, concat_axis=0, tiled=True)]
    all_to_all x3 -> x0, waiting for transfers between devices: 18.3 us -> none  [the longest x1 10.2 us: body(): lax.all_to_all(outgoing, 'ctx', split_axis=0, concat_axis=0, tiled=True)]
    reshape x7 -> x0, local copies, waits for them, and re-layouts: 8.35 us -> none  [the longest x1 3.28 us: body(): jnp.repeat(queries.reshape(tile_count, tile_len * row_width), pick_count,...]
    mul x2 -> x0, local copies, waits for them, and re-layouts: 6.77 us -> none  [combine(): own_weight[..., None] * own_out]
  transfers between devices with their start and end apart: 3 -> 0, of which waited for: 3 -> 0; matrix products, arithmetic and copies ran while one was open for 25% -> 0% of each run, Pallas kernels for 0% -> 0%
where the time goes in v1:
time: 96.2 us; the launch traced here: 96 us
  Pallas kernels  92 us (96%)
  local copies, waits for them, and re-layouts  4 us (4%)
    pallas_call x1, Pallas kernels, body(): pl.pallas_call(functools.partial(kernel, blocks, depth), out_shape=jax.Sh...  92 us
    unnamed x2, local copies, waits for them, and re-layouts  4 us

profile of v1, /device:TPU:2, one launch (start us, length us, event | category | flops | bytes accessed | tf_op | source)
XLA Modules:
  0.0 96.0 jit_solution(17980526345501418842)
XLA Ops:
  0.0 1.4 %copy.5.sel = s32[16,2]{1,0:T(8,128)} copy(s32[16,2]{0,1:T(2,128)} %param.7) | data formatting | bytes 256 | tf_op args[3]
  1.4 92.0 %shard_map.46 = bf16[96,8192]{1,0:T(8,128)(2,1)} custom-call(s32[16,2]{1,0:T(8,128)} %copy.5.sel, bf16[768,1024]{1,0:T(8,128)(2,1)} %q.1, bf16[768,1024]{1,0:T(8,128)(2,1)} %k_hbm.1, bf16[768,1024]{1,0:T(8,128)(2,1)} %v_hbm.1), custom_call_target="tpu_custom_call" | custom-call | tf_op jit(solution)/shard_map/pallas_call | solution.py:285
  93.4 2.7 %copy.7 = bf16[96,8192]{1,0:T(8,128)(2,1)} copy(bf16[96,8192]{1,0:T(8,128)(2,1)} %shard_map.46) | data formatting | bytes 3145728
